TPU v7x, 32 devices: a whole 2x2x4 slice. The times are simulated.
32 devices in a mesh: groups: 2 (over x), blk: 16 (over z, y, core).
Axes of the slice: x: 2, y: 2, z: 4, core: 2. Of those that a mesh axis runs over, the one named last changes fastest.
Arguments:
- hidden: bfloat16 [8192, 14336], P(('groups', 'blk')), parts along dimension 0, may hold values from -170 to 170
- cotangent: bfloat16 [8192, 4096], P(('groups', 'blk')), parts along dimension 0, may hold values from -170 to 170
- proj_in: bfloat16 [14336, 64], replicated, may hold values from -0.046875 to 0.046875
- proj_out: bfloat16 [4096, 64], replicated, may hold values from -0.09375 to 0.09375
- token_counts: int32 [128], P(('groups', 'blk')), parts along dimension 0, may hold values from 16 to 64
- loss_mask: int32 [8192], P(('groups', 'blk')), parts along dimension 0, may hold values 0 or 1
- prompt_ids: int32 [128], P('groups'), parts along dimension 0, may hold values from 0 to 15
Outputs:
- similarity: float32 [128, 64], P(('groups', 'blk')), parts along dimension 0
- self_norm: float32 [128], P(('groups', 'blk')), parts along dimension 0
- dup_score: float32 [128], P(('groups', 'blk')), parts along dimension 0
There are 2 independent parts, one for each index of `groups`. A program takes and returns all parts, laid end to end along the dimension named above; an argument that names none is the same for every part. Nothing has to cross between parts.
All inputs are finite; a program needn't handle non-finite values. No bound on the sum of `loss_mask` on one device may be relied on, other than what follows from the above.
Results may differ from a plain program's by a relative error of at most 0.012.
The roundings to bfloat16 on the way count: a program that leaves them out, or rounds other values in their place, can miss the bound.
Values may be sent and summed in bfloat16 or wider, within the bound.
A program may use at most 64 MiB of HBM per device.

v0:
```python
import jax
import jax.numpy as jnp
from jax import lax
from jax.sharding import PartitionSpec as P

HIGHEST_MODE = lax.Precision.HIGHEST
DAMPING = 0.05
EPSILON = 1e-06
ROW_CONTRACT = (((1,), (1,)), ((), ()))


def factor_inverses(act_cov, grad_cov):
    rank_width = act_cov.shape[0]
    inverses = []
    for cov_matrix in (act_cov, grad_cov):
        identity = jnp.eye(rank_width, dtype=cov_matrix.dtype)
        damped = cov_matrix + (DAMPING * jnp.trace(cov_matrix) / rank_width + EPSILON) * identity
        lower_factor = jnp.linalg.cholesky(damped)
        inverses.append(jax.scipy.linalg.solve_triangular(lower_factor, identity, lower=True))
    return (inverses[0], inverses[1])


def whiten(raw_blocks, inv_grad, inv_act):
    rank_width = inv_act.shape[0]
    count_rows = raw_blocks.shape[0]
    grad_blocks = raw_blocks.astype(jnp.float32).reshape(count_rows, rank_width, rank_width)
    left_side = jnp.einsum("ab,ebc->eac", inv_grad, grad_blocks, precision=HIGHEST_MODE)
    whitened = jnp.einsum("eac,dc->ead", left_side, inv_act, precision=HIGHEST_MODE)
    return whitened.reshape(count_rows, rank_width * rank_width).astype(jnp.bfloat16)


def local(hidden, cotangent, proj_in, proj_out, token_counts, loss_mask, prompt_ids):
    rank_width = proj_in.shape[1]
    ex_dev = token_counts.shape[0]
    tok_dev = hidden.shape[0]
    tok_ex = tok_dev // ex_dev
    devices = lax.axis_size("blk")
    my_index = lax.axis_index("blk")
    col_count = ex_dev * devices
    act_proj = jnp.dot(hidden, proj_in, preferred_element_type=jnp.float32)
    grad_proj = jnp.dot(cotangent, proj_out, preferred_element_type=jnp.float32)
    slot_place = jnp.arange(tok_ex, dtype=jnp.int32)
    valid_slot = (slot_place[None, :] < token_counts[:, None]).astype(jnp.float32).reshape(tok_dev)
    masked_act = act_proj * valid_slot[:, None]
    masked_grad = grad_proj * (valid_slot * loss_mask.astype(jnp.float32))[:, None]
    act_part = jnp.dot(masked_act.T, masked_act, precision=HIGHEST_MODE)
    grad_part = jnp.dot(masked_grad.T, masked_grad, precision=HIGHEST_MODE)
    row_scale = 1.0 / jnp.sqrt(rank_width * token_counts.astype(jnp.float32))
    outer_sum = jnp.einsum(
        "etk,etl->ekl",
        masked_grad.reshape(ex_dev, tok_ex, rank_width),
        act_proj.reshape(ex_dev, tok_ex, rank_width),
        precision=HIGHEST_MODE,
    )
    example_grad = (
        (outer_sum * row_scale[:, None, None])
        .astype(jnp.bfloat16)
        .reshape(ex_dev, rank_width * rank_width)
    )
    act_sum, grad_sum = lax.psum((act_part, grad_part), "blk")
    token_total = tok_dev * devices
    inv_act, inv_grad = factor_inverses(act_sum / token_total, grad_sum / token_total)
    own_blocks = whiten(example_grad, inv_grad, inv_act)
    row_block = lax.dot_general(
        own_blocks,
        lax.all_gather(own_blocks, "blk", axis=0, tiled=True),
        ROW_CONTRACT,
        preferred_element_type=jnp.float32,
    )
    row_start = my_index * ex_dev
    row_ids = row_start + jnp.arange(ex_dev, dtype=jnp.int32)
    col_ids = jnp.arange(col_count, dtype=jnp.int32)
    similarity = jnp.where(row_ids[:, None] == col_ids[None, :], 0.0, row_block)
    self_norm = jnp.sum(jnp.square(own_blocks.astype(jnp.float32)), axis=1) / rank_width
    own_prompts = lax.dynamic_slice_in_dim(prompt_ids, row_start, ex_dev)
    same_prompt = own_prompts[:, None] == prompt_ids[None, :]
    dup_score = jnp.sum(jnp.where(same_prompt, similarity * similarity, 0.0), axis=1)
    return (similarity, self_norm, dup_score)


def solution(mesh):
    placed = (
        P(("groups", "blk"), None),
        P(("groups", "blk"), None),
        P(),
        P(),
        P(("groups", "blk")),
        P(("groups", "blk")),
        P("groups"),
    )
    return jax.shard_map(
        local,
        mesh=mesh,
        in_specs=placed,
        out_specs=(P(("groups", "blk"), None), P(("groups", "blk")), P(("groups", "blk"))),
        check_vma=False,
    )
```

profile of v0, /device:TPU:1, one launch (start us, length us, event | category | flops | bytes accessed | tf_op | source)
XLA Modules:
  0.0 124.0 jit_solution(17560241609361324380)
XLA Ops:
  0.6 0.9 dynamic_slice.3
  1.5 0.7 multiply_rsqrt_fusion
  2.2 0.7 iota_compare_fusion.5
  3.0 0.8 convert_select_fusion
  3.8 1.8 %convolution_multiply_fusion.1 = f32[256,64]{0,1:T(8,128)S(1)} fusion(bf16[256,4096]{1,0:T(8,128)(2,1)S(1)} %copy-done, bf16[4096,64]{0,1:T(8,128)(2,1)} %param.13, f32[256]{0:T(256)S(1)} %convert_select_fusion), kind=kOutput, calls=%fused_computation.4 | convolution fusion | flops 134234112 | bytes 2688000 | tf_op jit(solution)/shard_map/dot_general | solution.py:41
  5.6 0.2 fusion.14
  5.9 5.4 %fusion.13 = f32[256,64]{0,1:T(8,128)S(1)} fusion(bf16[256,14336]{1,0:T(8,128)(2,1)} %param.10, bf16[14336,64]{0,1:T(8,128)(2,1)S(1)} %copy-done.1), kind=kOutput, calls=%fused_computation.43 | convolution fusion | flops 469762048 | bytes 9240576 | tf_op jit(solution)/shard_map/dot_general | solution.py:40
  11.3 0.2 fusion.2
  11.5 58.1 %all-reduce = (f32[64,64]{0,1:T(8,128)S(1)}, f32[64,64]{0,1:T(8,128)S(1)}) all-reduce(f32[64,64]{0,1:T(8,128)S(1)} %fusion.14, f32[64,64]{0,1:T(8,128)S(1)} %fusion.2), channel_id=1, replica_groups=mesh['groups'=2,'blk'=16] {'blk'}, use_global_device_ids=true, to_apply=%region_0.0 | all-reduce | flops 8192 | bytes 65536 | tf_op jit(solution)/shard_map/psum | solution.py:60
  69.6 0.6 select_reduce_fusion.2
  70.9 0.6 select_reduce_fusion.3
  72.2 5.8 %cholesky.55 = f32[64,64]{1,0:T(8,128)S(1)} custom-call(f32[64,64]{1,0:T(8,128)S(1)} %fusion.9), custom_call_target="Cholesky" | custom-call | tf_op jit(solution)/shard_map/jit(cholesky)/cholesky | solution.py:18
  78.1 0.6 compare_reduce_fusion
  78.8 0.7 fusion.7
  79.4 4.9 %custom-call.7 = f32[1,64,64]{1,2,0:T(8,128)S(1)} custom-call(f32[1,64,64]{2,1,0:T(8,128)S(1)} %fusion.7), custom_call_target="InvertDiagBlocksLowerTriangular" | custom-call | tf_op jit(solution)/shard_map/jit(_solve_triangular)/triangular_solve | solution.py:19
  84.3 0.3 convolution_bitcast_fusion.1
  84.7 5.8 %cholesky.44 = f32[64,64]{1,0:T(8,128)S(1)} custom-call(f32[64,64]{1,0:T(8,128)S(1)} %fusion.11), custom_call_target="Cholesky" | custom-call | tf_op jit(solution)/shard_map/jit(cholesky)/cholesky | solution.py:18
  90.6 0.6 compare_reduce_fusion.1
  91.2 0.7 fusion.6
  91.9 4.9 %custom-call.6 = f32[1,64,64]{1,2,0:T(8,128)S(1)} custom-call(f32[1,64,64]{2,1,0:T(8,128)S(1)} %fusion.6), custom_call_target="InvertDiagBlocksLowerTriangular" | custom-call | tf_op jit(solution)/shard_map/jit(_solve_triangular)/triangular_solve | solution.py:19
  96.8 0.3 convolution_bitcast_fusion.2
  97.0 0.1 copy.22
  97.1 0.1 reshape.52
  97.2 0.3 fusion
  97.5 0.2 convolution_bitcast_fusion
  97.7 0.4 multiply_reduce_fusion
  98.1 0.5 broadcast_multiply_fusion
  98.6 0.1 reshape.54
  98.7 0.1 convert_element_type.41
  98.8 23.6 %all-gather = bf16[16,4,4096]{2,1,0:T(4,128)(2,1)S(1)} all-gather(bf16[1,4,4096]{2,1,0:T(4,128)(2,1)S(1)} %reshape.54), channel_id=1, replica_groups=mesh['groups'=2,'blk'=16] {'blk'}, dimensions={0}, use_global_device_ids=true | all-gather | bytes 557056 | tf_op jit(solution)/shard_map/all_gather | solution.py:66
  122.4 0.1 reshape.55
  122.5 1.5 %select_reduce_fusion.4 = (f32[4]{0:T(128)}, f32[4,64]{1,0:T(4,128)}) fusion(s32[64]{0:T(128)S(1)} %copy-done.2, s32[4]{0:T(128)S(1)} %dynamic_slice.3, bf16[4,4096]{1,0:T(4,128)(2,1)S(1)} %convert_element_type.41, bf16[64,4096]{1,0:T(8,128)(2,1)S(1)} %reshape.55, s32[4]{0:T(128)S(1)} %iota_add_fusion), kind=kOutput, calls=%fused_computation.34 | convolution fusion | flops 2098684 | bytes 558384 | tf_op jit(solution)/shard_map/dot_general | solution.py:64
  (16 shorter events, 0.4 us)
Async XLA Ops:
  0.6 3.2 %copy-start = (bf16[256,4096]{1,0:T(8,128)(2,1)S(1)}, bf16[256,4096]{1,0:T(8,128)(2,1)}, u32[]{:S(2)}) copy-start(bf16[256,4096]{1,0:T(8,128)(2,1)} %param.11) | copy-start | bytes 6291460
  3.0 2.8 %copy-start.1 = (bf16[14336,64]{0,1:T(8,128)(2,1)S(1)}, bf16[14336,64]{0,1:T(8,128)(2,1)}, u32[]{:S(2)}) copy-start(bf16[14336,64]{0,1:T(8,128)(2,1)} %param.12) | copy-start | bytes 5505028
  11.3 111.2 %copy-start.2 = (s32[64]{0:T(128)S(1)}, s32[64]{0:T(128)}, u32[]{:S(2)}) copy-start(s32[64]{0:T(128)} %param.16) | copy-start | bytes 772
where the time goes:
time: 124 us
  blocking collectives  81.6 us (66%)
  other arithmetic  28.1 us (23%)
  matrix products  10.4 us (8%)
  between operations  2.11 us (2%)
  local copies, waits for them, and re-layouts  1.69 us (1%)
    psum x1, blocking collectives, local(): act_sum, grad_sum = lax.psum((act_part, grad_part), 'blk')  58.1 us
    all_gather x1, blocking collectives, local(): lax.all_gather(own_blocks, 'blk', axis=0, tiled=True)  23.6 us
    another operation x6, other arithmetic, factor_inverses(): lower_factor = jnp.linalg.cholesky(damped)  13 us
    another operation x4, other arithmetic, factor_inverses(): jax.scipy.linalg.solve_triangular(lower_factor, identity, lower=True)  11.1 us
    dot_general x1, matrix products, local(): act_proj = jnp.dot(hidden, proj_in, preferred_element_type=jnp.float32)  5.42 us

commit v1 on v0

v1 whole, which is shorter than its diff:
```python
import functools

import jax
import jax.numpy as jnp
from jax import lax
from jax.experimental import pallas as pl
from jax.experimental.pallas import tpu as pltpu
from jax.sharding import PartitionSpec as P

HIGHEST_MODE = lax.Precision.HIGHEST
DAMPING = 0.05
EPSILON = 1e-06
MESH = pl.DeviceIdType.MESH
NN = (((1,), (0,)), ((), ()))
NT = (((1,), (1,)), ((), ()))
TN = (((0,), (0,)), ((), ()))
BLOCK_ROWS = 16


def dot32(a, b, dims=NN):
    return lax.dot_general(a, b, dims, precision=HIGHEST_MODE, preferred_element_type=jnp.float32)


def fold(square):
    half = square.shape[0] // 2
    return jnp.concatenate([square[:half], square[half:]], axis=1)


def unfold(folded):
    width = folded.shape[1] // 2
    return jnp.concatenate([folded[:, :width], folded[:, width:]], axis=0)


def spd_inverse(cov):
    width = cov.shape[0]
    row = lax.broadcasted_iota(jnp.int32, cov.shape, 0)
    col = lax.broadcasted_iota(jnp.int32, cov.shape, 1)
    on_diag = row == col
    trace = jnp.sum(jnp.sum(jnp.where(on_diag, cov, 0.0), axis=1, keepdims=True), axis=0, keepdims=True)
    shift = DAMPING * trace / width + EPSILON
    scale = 1.0 / (trace + shift)
    ident = jnp.where(on_diag, 1.0, 0.0)
    ratio = (cov + shift * ident) * scale
    low = 0.96 * DAMPING / (width + DAMPING)
    step = 2.0 / (1.0 + low)
    inverse = step * (2.0 * ident - step * ratio)
    ratio = step * (2.0 * ratio - step * dot32(ratio, ratio))
    low = 4.0 * low / (1.0 + low) ** 2
    while True:
        step = 2.0 / (1.0 + low)
        low = 4.0 * low / (1.0 + low) ** 2
        if 1.0 - low < 1e-5:
            inverse = step * (2.0 * inverse - step * dot32(inverse, ratio))
            return inverse * scale
        both = jnp.concatenate([ratio, inverse], axis=0)
        both = step * (2.0 * both - step * dot32(both, ratio))
        ratio, inverse = both[:width], both[width:]


def kernel(
    n, chunk,
    hidden, cotangent, proj_in, proj_out, counts, prompts, loss_row, prompt_row,
    sim_out, norm_out, dup_out,
    hid_v, cot_v, pin_v, pout_v, packed, half_send, half_recv, slots, inv_send, inv_recv, grads,
    in_sem, half_sem, slot_send, slot_recv, inv_sem, own_sem, grad_send, grad_recv, fwd_send, fwd_recv,
):
    chips = n // 2
    me = lax.axis_index("blk")
    group = lax.axis_index("groups")
    chip, core = me // 2, me % 2
    sibling = me + 1 - 2 * core
    tok, wide = hidden.shape
    rank = proj_in.shape[0]
    ex = counts.shape[0]
    tok_ex = tok // ex
    half = rank // 2

    def peer(shift):
        return lax.rem(chip + shift, chips)

    loads = []
    for source, weight, source_v, weight_v in (
        (cotangent, proj_out, cot_v, pout_v),
        (hidden, proj_in, hid_v, pin_v),
    ):
        for start in range(0, source.shape[1], chunk):
            cols = pl.ds(start, min(chunk, source.shape[1] - start))
            pair = []
            for from_ref, to_ref in ((weight, weight_v), (source, source_v)):
                copy = pltpu.make_async_copy(from_ref.at[:, cols], to_ref.at[:, cols], in_sem.at[2 * len(loads) + len(pair)])
                copy.start()
                pair.append(copy)
            loads.append((pair, cols, source_v, weight_v))

    barrier = pltpu.get_barrier_semaphore()
    pl.semaphore_signal(barrier, inc=1, device_id=(group, sibling), device_id_type=MESH)

    @pl.loop(1, chips)
    def _(shift):
        pl.semaphore_signal(barrier, inc=1, device_id=(group, 2 * peer(shift) + core), device_id_type=MESH)

    grad_t = jnp.zeros((rank, tok), jnp.float32)
    act = jnp.zeros((tok, rank), jnp.float32)
    for pair, cols, source_v, weight_v in loads:
        for copy in pair:
            copy.wait()
        if source_v is cot_v:
            grad_t += lax.dot_general(weight_v[:, cols], source_v[:, cols], NT, preferred_element_type=jnp.float32)
        else:
            act += lax.dot_general(source_v[:, cols], weight_v[:, cols], NT, preferred_element_type=jnp.float32)

    lane_tok = lax.broadcasted_iota(jnp.int32, (1, tok), 1)
    sub_tok = lax.broadcasted_iota(jnp.int32, (tok, 1), 0)
    lane_end = jnp.zeros((1, tok), jnp.int32)
    sub_end = jnp.zeros((tok, 1), jnp.int32)
    for e in range(ex):
        end = e * tok_ex + counts[e]
        lane_end = jnp.where(lane_tok // tok_ex == e, end, lane_end)
        sub_end = jnp.where(sub_tok // tok_ex == e, end, sub_end)
    lane_keep = jnp.where(lane_tok < lane_end, loss_row[...].astype(jnp.float32), 0.0)
    masked_grad = grad_t * lane_keep
    masked_act = jnp.where(sub_tok < sub_end, act, 0.0)

    act_part = fold(dot32(masked_act, masked_act, TN))
    grad_part = fold(dot32(masked_grad, masked_grad, NT))
    half_send[...] = jnp.where(core == 0, grad_part, act_part)
    pl.semaphore_wait(barrier, chips)
    half_copy = pltpu.make_async_remote_copy(
        src_ref=half_send, dst_ref=half_recv, send_sem=half_sem.at[0], recv_sem=half_sem.at[1],
        device_id=(group, sibling), device_id_type=MESH)
    half_copy.start()

    halves = []
    for h in range(2):
        rows = [
            jnp.where(lane_tok // tok_ex == e, masked_grad[h * half:(h + 1) * half], 0.0)
            for e in range(ex)
        ]
        summed = dot32(jnp.concatenate(rows, axis=0), act)
        parts = []
        for e in range(ex):
            count = jnp.full((1, 1), counts[e], jnp.int32).astype(jnp.float32)
            parts.append(summed[e * half:(e + 1) * half] * (1.0 / jnp.sqrt(rank * count)))
        halves.append(jnp.concatenate(parts, axis=0).astype(jnp.bfloat16).astype(jnp.float32))
    packed[...] = jnp.concatenate(halves, axis=1)
    per = BLOCK_ROWS // ex
    count_blocks = half // per

    def flat_rows():
        return jnp.concatenate(
            [packed[pl.ds(b, BLOCK_ROWS, stride=count_blocks), :] for b in range(count_blocks)], axis=1)

    own_rows = pl.ds(pl.multiple_of(me * BLOCK_ROWS, BLOCK_ROWS), BLOCK_ROWS)
    grads[own_rows, :] = flat_rows().astype(jnp.bfloat16)

    half_copy.wait()
    slots[chip] = jnp.where(core == 0, act_part, grad_part) + half_recv[...]

    def slot_copy(shift, source_chip, send, recv):
        return pltpu.make_async_remote_copy(
            src_ref=slots.at[source_chip], dst_ref=slots.at[source_chip], send_sem=send, recv_sem=recv,
            device_id=(group, 2 * peer(shift) + core), device_id_type=MESH)

    def grad_copy(owner, target, send, recv):
        rows = pl.ds(pl.multiple_of(owner * BLOCK_ROWS, BLOCK_ROWS), BLOCK_ROWS)
        return pltpu.make_async_remote_copy(
            src_ref=grads.at[rows, :], dst_ref=grads.at[rows, :], send_sem=send, recv_sem=recv,
            device_id=(group, target), device_id_type=MESH)

    @pl.loop(1, chips)
    def _(shift):
        slot_copy(shift, chip, slot_send.at[shift], slot_recv.at[shift]).start()

    grad_copy(me, sibling, own_sem.at[0], own_sem.at[1]).start()

    @pl.loop(1, chips)
    def _(shift):
        grad_copy(me, 2 * peer(shift) + core, grad_send.at[shift], grad_recv.at[shift]).start()

    @pl.loop(1, chips)
    def _(shift):
        slot_copy(shift, peer(chips - shift), slot_send.at[shift], slot_recv.at[shift]).wait_recv()

    total = slots[0]
    for k in range(1, chips):
        total += slots[k]
    tokens = tok * n
    inv_own = spd_inverse(unfold(total) * (1.0 / tokens))
    inv_send[...] = fold(inv_own)
    inv_copy = pltpu.make_async_remote_copy(
        src_ref=inv_send, dst_ref=inv_recv, send_sem=inv_sem.at[0], recv_sem=inv_sem.at[1],
        device_id=(group, sibling), device_id_type=MESH)
    inv_copy.start()

    @pl.loop(1, chips)
    def _(shift):
        owner = 2 * peer(chips - shift) + core
        grad_copy(owner, sibling, grad_send.at[shift], grad_recv.at[shift]).wait_recv()
        grad_copy(owner, sibling, fwd_send.at[shift], fwd_recv.at[shift]).start()

    inv_copy.wait()
    inv_other = unfold(inv_recv[...])
    inv_act = jnp.where(core == 0, inv_own, inv_other)
    inv_grad = jnp.where(core == 0, inv_other, inv_own)
    sides = [dot32(part, inv_act) for part in halves]
    for e in range(ex):
        rows = slice(e * half, (e + 1) * half)
        both = jnp.concatenate([sides[0][rows], sides[1][rows]], axis=0)
        packed[rows, :] = fold(dot32(inv_grad, both))
    scaled = flat_rows()
    terms = []
    for _ in range(3):
        term = scaled.astype(jnp.bfloat16)
        scaled = scaled - term.astype(jnp.float32)
        terms.append(term)
    lhs = jnp.concatenate(terms, axis=0)

    grad_copy(sibling, sibling, own_sem.at[0], own_sem.at[1]).wait_recv()

    @pl.loop(1, chips)
    def _(shift):
        owner = 2 * peer(chips - shift) + 1 - core
        grad_copy(owner, sibling, fwd_send.at[shift], fwd_recv.at[shift]).wait_recv()

    cross = lax.dot_general(lhs, grads[...], NT, preferred_element_type=jnp.float32)
    cross = cross[:BLOCK_ROWS] + cross[BLOCK_ROWS:2 * BLOCK_ROWS] + cross[2 * BLOCK_ROWS:]
    lanes = n * BLOCK_ROWS
    row = lax.broadcasted_iota(jnp.int32, (BLOCK_ROWS, lanes), 0)
    col = lax.broadcasted_iota(jnp.int32, (BLOCK_ROWS, lanes), 1)
    cross = jnp.where(row % per == col % per, cross, 0.0)
    cols_all = n * ex
    pick_row = lax.broadcasted_iota(jnp.int32, (lanes, cols_all), 0)
    pick_col = lax.broadcasted_iota(jnp.int32, (lanes, cols_all), 1)
    by_chunk = dot32(cross, jnp.where(pick_row // per == pick_col, 1.0, 0.0))
    products = jnp.concatenate(
        [jnp.sum(by_chunk[e * per:(e + 1) * per], axis=0, keepdims=True) for e in range(ex)], axis=0)

    row_ids = me * ex + lax.broadcasted_iota(jnp.int32, (ex, cols_all), 0)
    col_ids = lax.broadcasted_iota(jnp.int32, (ex, cols_all), 1)
    diagonal = row_ids == col_ids
    similarity = jnp.where(diagonal, 0.0, products)
    sim_out[...] = similarity
    norm_col = jnp.sum(jnp.where(diagonal, products, 0.0), axis=1, keepdims=True) / rank
    own_prompt = jnp.concatenate(
        [jnp.full((1, cols_all), prompts[me * ex + e], jnp.int32) for e in range(ex)], axis=0)
    same = own_prompt == prompt_row[...]
    dup_col = jnp.sum(jnp.where(same, similarity * similarity, 0.0), axis=1, keepdims=True)
    small_row = lax.broadcasted_iota(jnp.int32, (ex, ex), 0)
    small_col = lax.broadcasted_iota(jnp.int32, (ex, ex), 1)
    norm_out[...] = jnp.sum(jnp.where(small_row == small_col, norm_col, 0.0), axis=0, keepdims=True)
    dup_out[...] = jnp.sum(jnp.where(small_row == small_col, dup_col, 0.0), axis=0, keepdims=True)

    grad_copy(me, sibling, own_sem.at[0], own_sem.at[1]).wait_send()

    @pl.loop(1, chips)
    def _(shift):
        slot_copy(shift, chip, slot_send.at[shift], slot_recv.at[shift]).wait_send()
        grad_copy(me, 2 * peer(shift) + core, grad_send.at[shift], grad_recv.at[shift]).wait_send()
        owner = 2 * peer(chips - shift) + core
        grad_copy(owner, sibling, fwd_send.at[shift], fwd_recv.at[shift]).wait_send()


def local(n, hidden, cotangent, proj_in, proj_out, token_counts, loss_mask, prompt_ids):
    tok, wide = hidden.shape
    model = cotangent.shape[1]
    rank = proj_in.shape[1]
    ex = token_counts.shape[0]
    chips = n // 2
    chunk = 2048
    loads = -(-wide // chunk) + -(-model // chunk)
    folded = (rank // 2, 2 * rank)
    dma = pltpu.SemaphoreType.DMA
    f32, bf16 = jnp.float32, jnp.bfloat16
    whole = pl.BlockSpec(memory_space=pltpu.VMEM)
    scalars = pl.BlockSpec(memory_space=pltpu.SMEM)
    far = pl.BlockSpec(memory_space=pltpu.HBM)
    similarity, self_norm, dup_score = pl.pallas_call(
        functools.partial(kernel, n, chunk),
        out_shape=(
            jax.ShapeDtypeStruct((ex, n * ex), f32),
            jax.ShapeDtypeStruct((1, ex), f32),
            jax.ShapeDtypeStruct((1, ex), f32),
        ),
        in_specs=[far, far, far, far, scalars, scalars, whole, whole],
        out_specs=(whole, whole, whole),
        scratch_shapes=[
            pltpu.VMEM((tok, wide), bf16),
            pltpu.VMEM((tok, model), bf16),
            pltpu.VMEM((rank, wide), bf16),
            pltpu.VMEM((rank, model), bf16),
            pltpu.VMEM((ex * rank // 2, 2 * rank), f32),
            pltpu.VMEM(folded, f32),
            pltpu.VMEM(folded, f32),
            pltpu.VMEM((chips,) + folded, f32),
            pltpu.VMEM(folded, f32),
            pltpu.VMEM(folded, f32),
            pltpu.VMEM((n * BLOCK_ROWS, ex * rank * rank // BLOCK_ROWS), bf16),
            dma((2 * loads,)), dma((2,)), dma((chips,)), dma((chips,)), dma((2,)), dma((2,)),
            dma((chips,)), dma((chips,)), dma((chips,)), dma((chips,)),
        ],
        compiler_params=pltpu.CompilerParams(
            collective_id=0, has_side_effects=True, vmem_limit_bytes=48 * 1024 * 1024),
        cost_estimate=pl.CostEstimate(
            flops=2 * tok * (wide + model) * rank, bytes_accessed=2 * tok * (wide + model), transcendentals=0),
    )(hidden, cotangent, proj_in.T, proj_out.T, token_counts, prompt_ids,
      loss_mask.reshape(1, tok), prompt_ids.reshape(1, n * ex))
    return similarity, self_norm.reshape(ex), dup_score.reshape(ex)


def solution(mesh):
    placed = (
        P(("groups", "blk"), None),
        P(("groups", "blk"), None),
        P(),
        P(),
        P(("groups", "blk")),
        P(("groups", "blk")),
        P("groups"),
    )
    return jax.shard_map(
        functools.partial(local, mesh.shape["blk"]),
        mesh=mesh,
        in_specs=placed,
        out_specs=(P(("groups", "blk"), None), P(("groups", "blk")), P(("groups", "blk"))),
        check_vma=False,
    )
```

time: 124 us -> 31.4 us (0.25)
  blocking collectives: 81.6 us -> 0 us
  other arithmetic: 28.1 us -> 0 us
  Pallas kernels: 0 us -> 22.8 us
  matrix products: 10.4 us -> 0 us
  local copies, waits for them, and re-layouts: 1.69 us -> 7.71 us
  between operations: 2.11 us -> 0.66 us
    psum x1 -> x0, blocking collectives: 58.1 us -> none  [local(): act_sum, grad_sum = lax.psum((act_part, grad_part), 'blk')]
    another operation x10 -> x0, other arithmetic: 24.1 us -> none  [the longest x6 13 us: factor_inverses(): lower_factor = jnp.linalg.cholesky(damped)]
    all_gather x1 -> x0, blocking collectives: 23.6 us -> none  [local(): lax.all_gather(own_blocks, 'blk', axis=0, tiled=True)]
    pallas_call x0 -> x1, Pallas kernels: none -> 22.8 us  [local(): pl.pallas_call(functools.partial(kernel, n, chunk), out_shape=(jax.ShapeD...]
    dot_general x8 -> x0, matrix products: 9.89 us -> none  [the longest x1 5.42 us: local(): act_proj = jnp.dot(hidden, proj_in, preferred_element_type=jnp.float32)]
    unnamed x8 -> x15, local copies, waits for them, and re-layouts: 0.25 us -> 7.71 us
where the time goes in v1:
time: 31.4 us; the launch traced here: 31.1 us
  Pallas kernels  22.8 us (73%)
  local copies, waits for them, and re-layouts  7.71 us (25%)
  between operations  0.66 us (2%)
    pallas_call x1, Pallas kernels, local(): pl.pallas_call(functools.partial(kernel, n, chunk), out_shape=(jax.ShapeD...  22.8 us
    unnamed x15, local copies, waits for them, and re-layouts  7.71 us

profile of v1, /device:TPU:1, one launch (start us, length us, event | category | flops | bytes accessed | tf_op | source)
XLA Modules:
  0.0 31.1 jit_solution(4426828894386657269)
XLA Ops:
  0.6 0.0 copy-start
  0.6 1.6 %copy-done = bf16[256,4096]{1,0:T(8,128)(2,1)S(1)} copy-done((bf16[256,4096]{1,0:T(8,128)(2,1)S(1)}, bf16[256,4096]{1,0:T(8,128)(2,1)}, u32[]{:S(2)}) %copy-start) | copy-done | bytes 2097176
  2.2 0.0 copy-start.1
  2.2 1.5 %copy-done.1 = bf16[14336,64]{0,1:T(8,128)(2,1)S(1)} copy-done((bf16[14336,64]{0,1:T(8,128)(2,1)S(1)}, bf16[14336,64]{0,1:T(8,128)(2,1)}, u32[]{:S(2)}) %copy-start.1) | copy-done | bytes 1835032
  3.7 0.0 copy-start.2
  3.7 1.0 %copy-done.2 = bf16[4096,64]{0,1:T(8,128)(2,1)S(1)} copy-done((bf16[4096,64]{0,1:T(8,128)(2,1)S(1)}, bf16[4096,64]{0,1:T(8,128)(2,1)}, u32[]{:S(2)}) %copy-start.2) | copy-done | bytes 524312
  4.8 0.0 copy-start.3
  4.8 0.7 %copy-done.3 = s32[64]{0:T(128)S(1)} copy-done((s32[64]{0:T(128)S(1)}, s32[64]{0:T(128)}, u32[]{:S(2)}) %copy-start.3) | copy-done | bytes 280
  5.4 0.0 copy-start.4
  5.4 0.7 %copy-done.4 = s32[256]{0:T(256)S(1)} copy-done((s32[256]{0:T(256)S(1)}, s32[256]{0:T(256)}, u32[]{:S(2)}) %copy-start.4) | copy-done | bytes 1048
  6.1 0.0 copy-start.5
  6.1 0.7 %copy-done.5 = s32[4]{0:T(128)S(1)} copy-done((s32[4]{0:T(128)S(1)}, s32[4]{0:T(128)}, u32[]{:S(2)}) %copy-start.5) | copy-done | bytes 40
  6.8 22.8 %shard_map.94 = (f32[4,64]{1,0:T(4,128)S(1)}, f32[1,4]{1,0:T(1,128)S(1)}, f32[1,4]{1,0:T(1,128)S(1)}) custom-call(bf16[256,14336]{1,0:T(8,128)(2,1)} %hidden.1, bf16[256,4096]{1,0:T(8,128)(2,1)S(1)} %copy-done, bf16[64,14336]{1,0:T(8,128)(2,1)S(1)} %bitcast.6, bf16[64,4096]{1,0:T(8,128)(2,1)S(1)} %bitcast.7, s32[4]{0:T(128)S(1)} %copy-done.5, ...), custom_call_target="tpu_custom_call" | custom-call | flops 603979776 | bytes 9437184 | tf_op jit(solution)/shard_map/pallas_call | solution.py:277
  29.5 0.6 %copy.13 = f32[4,64]{1,0:T(4,128)} copy(f32[4,64]{1,0:T(4,128)S(1)} %get-tuple-element.12) | data formatting | bytes 2048
  30.1 0.5 %copy.14 = f32[4]{0:T(128)} copy(f32[4]{0:T(128)S(1)} %bitcast.11) | data formatting | bytes 32
  30.6 0.5 %copy.15 = f32[4]{0:T(128)} copy(f32[4]{0:T(128)S(1)} %bitcast.10) | data formatting | bytes 32
Async XLA Ops:
  0.6 1.6 %copy-start = (bf16[256,4096]{1,0:T(8,128)(2,1)S(1)}, bf16[256,4096]{1,0:T(8,128)(2,1)}, u32[]{:S(2)}) copy-start(bf16[256,4096]{1,0:T(8,128)(2,1)} %cotangent.1) | copy-start | bytes 6291460
  2.2 1.5 %copy-start.1 = (bf16[14336,64]{0,1:T(8,128)(2,1)S(1)}, bf16[14336,64]{0,1:T(8,128)(2,1)}, u32[]{:S(2)}) copy-start(bf16[14336,64]{0,1:T(8,128)(2,1)} %param.9) | copy-start | bytes 5505028
  3.7 1.0 %copy-start.2 = (bf16[4096,64]{0,1:T(8,128)(2,1)S(1)}, bf16[4096,64]{0,1:T(8,128)(2,1)}, u32[]{:S(2)}) copy-start(bf16[4096,64]{0,1:T(8,128)(2,1)} %param.10) | copy-start | bytes 1572868
  4.8 0.7 %copy-start.3 = (s32[64]{0:T(128)S(1)}, s32[64]{0:T(128)}, u32[]{:S(2)}) copy-start(s32[64]{0:T(128)} %prompts.1) | copy-start | bytes 772
  5.4 0.7 %copy-start.4 = (s32[256]{0:T(256)S(1)}, s32[256]{0:T(256)}, u32[]{:S(2)}) copy-start(s32[256]{0:T(256)} %param.12) | copy-start | bytes 3076
  6.1 0.7 %copy-start.5 = (s32[4]{0:T(128)S(1)}, s32[4]{0:T(128)}, u32[]{:S(2)}) copy-start(s32[4]{0:T(128)} %counts.1) | copy-start | bytes 52

commit v2 on v1

--- a/solution.py
+++ b/solution.py
@@ -59,10 +59,11 @@
 
 def kernel(
     n, chunk,
-    hidden, cotangent, proj_in, proj_out, counts, prompts, loss_row, prompt_row,
+    hidden, cotangent, proj_in, proj_out, counts_far, loss_far, prompts_far,
     sim_out, norm_out, dup_out,
     hid_v, cot_v, pin_v, pout_v, packed, half_send, half_recv, slots, inv_send, inv_recv, grads,
-    in_sem, half_sem, slot_send, slot_recv, inv_sem, own_sem, grad_send, grad_recv, fwd_send, fwd_recv,
+    counts, prompts, loss_row, prompt_row,
+    in_sem, small_sem, half_sem, slot_send, slot_recv, inv_sem, own_sem, grad_send, grad_recv, fwd_send, fwd_recv,
 ):
     chips = n // 2
     me = lax.axis_index("blk")
@@ -71,7 +72,7 @@
     sibling = me + 1 - 2 * core
     tok, wide = hidden.shape
     rank = proj_in.shape[0]
-    ex = counts.shape[0]
+    ex = counts_far.shape[0]
     tok_ex = tok // ex
     half = rank // 2
 
@@ -92,6 +93,14 @@
                 pair.append(copy)
             loads.append((pair, cols, source_v, weight_v))
 
+    small = []
+    for from_ref, to_ref in (
+        (counts_far, counts), (loss_far, loss_row.at[0]), (prompts_far, prompts), (prompts_far, prompt_row.at[0]),
+    ):
+        copy = pltpu.make_async_copy(from_ref, to_ref, small_sem.at[len(small)])
+        copy.start()
+        small.append(copy)
+
     barrier = pltpu.get_barrier_semaphore()
     pl.semaphore_signal(barrier, inc=1, device_id=(group, sibling), device_id_type=MESH)
 
@@ -109,6 +118,8 @@
         else:
             act += lax.dot_general(source_v[:, cols], weight_v[:, cols], NT, preferred_element_type=jnp.float32)
 
+    for copy in small:
+        copy.wait()
     lane_tok = lax.broadcasted_iota(jnp.int32, (1, tok), 1)
     sub_tok = lax.broadcasted_iota(jnp.int32, (tok, 1), 0)
     lane_end = jnp.zeros((1, tok), jnp.int32)
@@ -272,7 +283,6 @@
     dma = pltpu.SemaphoreType.DMA
     f32, bf16 = jnp.float32, jnp.bfloat16
     whole = pl.BlockSpec(memory_space=pltpu.VMEM)
-    scalars = pl.BlockSpec(memory_space=pltpu.SMEM)
     far = pl.BlockSpec(memory_space=pltpu.HBM)
     similarity, self_norm, dup_score = pl.pallas_call(
         functools.partial(kernel, n, chunk),
@@ -281,7 +291,7 @@
             jax.ShapeDtypeStruct((1, ex), f32),
             jax.ShapeDtypeStruct((1, ex), f32),
         ),
-        in_specs=[far, far, far, far, scalars, scalars, whole, whole],
+        in_specs=[far] * 7,
         out_specs=(whole, whole, whole),
         scratch_shapes=[
             pltpu.VMEM((tok, wide), bf16),
@@ -295,15 +305,18 @@
             pltpu.VMEM(folded, f32),
             pltpu.VMEM(folded, f32),
             pltpu.VMEM((n * BLOCK_ROWS, ex * rank * rank // BLOCK_ROWS), bf16),
-            dma((2 * loads,)), dma((2,)), dma((chips,)), dma((chips,)), dma((2,)), dma((2,)),
+            pltpu.SMEM((ex,), jnp.int32),
+            pltpu.SMEM((n * ex,), jnp.int32),
+            pltpu.VMEM((1, tok), jnp.int32),
+            pltpu.VMEM((1, n * ex), jnp.int32),
+            dma((2 * loads,)), dma((4,)), dma((2,)), dma((chips,)), dma((chips,)), dma((2,)), dma((2,)),
             dma((chips,)), dma((chips,)), dma((chips,)), dma((chips,)),
         ],
         compiler_params=pltpu.CompilerParams(
-            collective_id=0, has_side_effects=True, vmem_limit_bytes=48 * 1024 * 1024),
+            collective_id=0, has_side_effects=True, vmem_limit_bytes=60 * 1024 * 1024),
         cost_estimate=pl.CostEstimate(
             flops=2 * tok * (wide + model) * rank, bytes_accessed=2 * tok * (wide + model), transcendentals=0),
-    )(hidden, cotangent, proj_in.T, proj_out.T, token_counts, prompt_ids,
-      loss_mask.reshape(1, tok), prompt_ids.reshape(1, n * ex))
+    )(hidden, cotangent, proj_in.T, proj_out.T, token_counts, loss_mask, prompt_ids)
     return similarity, self_norm.reshape(ex), dup_score.reshape(ex)
 
 

time: 31.4 us -> 28.4 us (0.904)
  local copies, waits for them, and re-layouts: 7.71 us -> 3.56 us
  Pallas kernels: 22.8 us -> 24 us
    unnamed x15 -> x3, local copies, waits for them, and re-layouts: 7.71 us -> 3.56 us
    pallas_call x1, Pallas kernels: 22.8 us -> 24 us  [local(): pl.pallas_call(functools.partial(kernel, n, chunk), out_shape=(jax.ShapeD...]
where the time goes in v2:
time: 28.4 us; the launch traced here: 28.2 us
  Pallas kernels  24 us (85%)
  local copies, waits for them, and re-layouts  3.56 us (13%)
  between operations  0.64 us (2%)
    pallas_call x1, Pallas kernels, local(): pl.pallas_call(functools.partial(kernel, n, chunk), out_shape=(jax.ShapeD...  24 us
    unnamed x3, local copies, waits for them, and re-layouts  3.56 us

profile of v2, /device:TPU:1, one launch (start us, length us, event | category | flops | bytes accessed | tf_op | source)
XLA Modules:
  0.0 28.2 jit_solution(15604954007043573703)
XLA Ops:
  0.6 24.0 %shard_map.94 = (f32[4,64]{1,0:T(4,128)}, f32[1,4]{1,0:T(1,128)}, f32[1,4]{1,0:T(1,128)}) custom-call(bf16[256,14336]{1,0:T(8,128)(2,1)} %hidden.1, bf16[256,4096]{1,0:T(8,128)(2,1)} %cotangent.1, bf16[64,14336]{1,0:T(8,128)(2,1)} %bitcast.4, bf16[64,4096]{1,0:T(8,128)(2,1)} %bitcast.5, s32[4]{0:T(128)} %counts_far.1, s32[256]{0:T(256)} %loss_far.1, ...), custom_call_target="tpu_custom_call" | custom-call | flops 603979776 | bytes 9437184 | tf_op jit(solution)/shard_map/pallas_call | solution.py:287
  24.7 1.2 %copy.13 = f32[4,64]{1,0:T(4,128)} copy(f32[4,64]{1,0:T(4,128)} %get-tuple-element.12) | data formatting | bytes 2048
  25.9 1.1 %copy.14 = f32[4]{0:T(128)} copy(f32[4]{0:T(128)} %bitcast.7) | data formatting | bytes 32
  27.1 1.2 %copy.15 = f32[4]{0:T(128)} copy(f32[4]{0:T(128)} %bitcast.6) | data formatting | bytes 32

commit v3 on v2

--- a/solution.py
+++ b/solution.py
@@ -313,10 +313,11 @@
             dma((chips,)), dma((chips,)), dma((chips,)), dma((chips,)),
         ],
         compiler_params=pltpu.CompilerParams(
-            collective_id=0, has_side_effects=True, vmem_limit_bytes=60 * 1024 * 1024),
+            collective_id=0, has_side_effects=True, vmem_limit_bytes=48 * 1024 * 1024),
         cost_estimate=pl.CostEstimate(
             flops=2 * tok * (wide + model) * rank, bytes_accessed=2 * tok * (wide + model), transcendentals=0),
-    )(hidden, cotangent, proj_in.T, proj_out.T, token_counts, loss_mask, prompt_ids)
+    )(*[pltpu.with_memory_space_constraint(x, pltpu.HBM) for x in (
+        hidden, cotangent, proj_in.T, proj_out.T, token_counts, loss_mask, prompt_ids)])
     return similarity, self_norm.reshape(ex), dup_score.reshape(ex)
 
 

time: 28.4 us -> 25.8 us (0.908)
  local copies, waits for them, and re-layouts: 3.56 us -> 1.6 us
  Pallas kernels: 24 us -> 23.4 us
    unnamed x3, local copies, waits for them, and re-layouts: 3.56 us -> 1.6 us
    pallas_call x1, Pallas kernels: 24 us -> 23.4 us  [local(): pl.pallas_call(functools.partial(kernel, n, chunk), out_shape=(jax.ShapeD...]
where the time goes in v3:
time: 25.8 us; the launch traced here: 25.7 us
  Pallas kernels  23.4 us (91%)
  local copies, waits for them, and re-layouts  1.6 us (6%)
  between operations  0.64 us (2%)
    pallas_call x1, Pallas kernels, local(): pl.pallas_call(functools.partial(kernel, n, chunk), out_shape=(jax.ShapeD...  23.4 us
    unnamed x3, local copies, waits for them, and re-layouts  1.6 us

profile of v3, /device:TPU:1, one launch (start us, length us, event | category | flops | bytes accessed | tf_op | source)
XLA Modules:
  0.0 25.7 jit_solution(4943190659591069233)
XLA Ops:
  0.6 23.4 %shard_map.94 = (f32[4,64]{1,0:T(4,128)S(1)}, f32[1,4]{1,0:T(1,128)S(1)}, f32[1,4]{1,0:T(1,128)S(1)}) custom-call(bf16[256,14336]{1,0:T(8,128)(2,1)} %hidden.1, bf16[256,4096]{1,0:T(8,128)(2,1)} %cotangent.1, bf16[64,14336]{1,0:T(8,128)(2,1)} %bitcast.6, bf16[64,4096]{1,0:T(8,128)(2,1)} %bitcast.7, s32[4]{0:T(128)} %counts_far.1, s32[256]{0:T(256)} %loss_far.1, ...), custom_call_target="tpu_custom_call" | custom-call | flops 603979776 | bytes 9437184 | tf_op jit(solution)/shard_map/pallas_call | solution.py:287
  24.1 0.6 %copy.13 = f32[4,64]{1,0:T(4,128)} copy(f32[4,64]{1,0:T(4,128)S(1)} %get-tuple-element.12) | data formatting | bytes 2048
  24.6 0.5 %copy.14 = f32[4]{0:T(128)} copy(f32[4]{0:T(128)S(1)} %bitcast.5) | data formatting | bytes 32
  25.2 0.5 %copy.15 = f32[4]{0:T(128)} copy(f32[4]{0:T(128)S(1)} %bitcast.4) | data formatting | bytes 32

commit v4 on v3

--- a/solution.py
+++ b/solution.py
@@ -15,6 +15,11 @@
 NT = (((1,), (1,)), ((), ()))
 TN = (((0,), (0,)), ((), ()))
 BLOCK_ROWS = 16
+SHARE_AFTER = 2
+
+
+def plan(length, chunk):
+    return [(start, min(chunk, length - start)) for start in range(0, length, chunk)]
 
 
 def dot32(a, b, dims=NN):
@@ -60,7 +65,7 @@
 def kernel(
     n, chunk,
     hidden, cotangent, proj_in, proj_out, counts_far, loss_far, prompts_far,
-    sim_out, norm_out, dup_out,
+    result,
     hid_v, cot_v, pin_v, pout_v, packed, half_send, half_recv, slots, inv_send, inv_recv, grads,
     counts, prompts, loss_row, prompt_row,
     in_sem, small_sem, half_sem, slot_send, slot_recv, inv_sem, own_sem, grad_send, grad_recv, fwd_send, fwd_recv,
@@ -84,8 +89,8 @@
         (cotangent, proj_out, cot_v, pout_v),
         (hidden, proj_in, hid_v, pin_v),
     ):
-        for start in range(0, source.shape[1], chunk):
-            cols = pl.ds(start, min(chunk, source.shape[1] - start))
+        for start, size in plan(source.shape[1], chunk):
+            cols = pl.ds(start, size)
             pair = []
             for from_ref, to_ref in ((weight, weight_v), (source, source_v)):
                 copy = pltpu.make_async_copy(from_ref.at[:, cols], to_ref.at[:, cols], in_sem.at[2 * len(loads) + len(pair)])
@@ -108,15 +113,29 @@
     def _(shift):
         pl.semaphore_signal(barrier, inc=1, device_id=(group, 2 * peer(shift) + core), device_id_type=MESH)
 
+    half_copy = pltpu.make_async_remote_copy(
+        src_ref=half_send, dst_ref=half_recv, send_sem=half_sem.at[0], recv_sem=half_sem.at[1],
+        device_id=(group, sibling), device_id_type=MESH)
+
+    def slot_copy(shift, source_chip, send, recv):
+        return pltpu.make_async_remote_copy(
+            src_ref=slots.at[source_chip], dst_ref=slots.at[source_chip], send_sem=send, recv_sem=recv,
+            device_id=(group, 2 * peer(shift) + core), device_id_type=MESH)
+
+    def share(part):
+        half_copy.wait_recv()
+        slots[chip] = part + half_recv[...]
+
+        @pl.loop(1, chips)
+        def _(shift):
+            slot_copy(shift, chip, slot_send.at[shift], slot_recv.at[shift]).start()
+
     grad_t = jnp.zeros((rank, tok), jnp.float32)
-    act = jnp.zeros((tok, rank), jnp.float32)
     for pair, cols, source_v, weight_v in loads:
-        for copy in pair:
-            copy.wait()
         if source_v is cot_v:
+            for copy in pair:
+                copy.wait()
             grad_t += lax.dot_general(weight_v[:, cols], source_v[:, cols], NT, preferred_element_type=jnp.float32)
-        else:
-            act += lax.dot_general(source_v[:, cols], weight_v[:, cols], NT, preferred_element_type=jnp.float32)
 
     for copy in small:
         copy.wait()
@@ -130,16 +149,34 @@
         sub_end = jnp.where(sub_tok // tok_ex == e, end, sub_end)
     lane_keep = jnp.where(lane_tok < lane_end, loss_row[...].astype(jnp.float32), 0.0)
     masked_grad = grad_t * lane_keep
+    grad_part = fold(dot32(masked_grad, masked_grad, NT))
+    pl.semaphore_wait(barrier, chips)
+
+    @pl.when(core == 0)
+    def _():
+        half_send[...] = grad_part
+        half_copy.start()
+
+    act = jnp.zeros((tok, rank), jnp.float32)
+    count_hidden = 0
+    for pair, cols, source_v, weight_v in loads:
+        if source_v is hid_v:
+            for copy in pair:
+                copy.wait()
+            act += lax.dot_general(source_v[:, cols], weight_v[:, cols], NT, preferred_element_type=jnp.float32)
+            count_hidden += 1
+            if count_hidden == SHARE_AFTER:
+                @pl.when(core == 1)
+                def _():
+                    share(grad_part)
+
     masked_act = jnp.where(sub_tok < sub_end, act, 0.0)
-
     act_part = fold(dot32(masked_act, masked_act, TN))
-    grad_part = fold(dot32(masked_grad, masked_grad, NT))
-    half_send[...] = jnp.where(core == 0, grad_part, act_part)
-    pl.semaphore_wait(barrier, chips)
-    half_copy = pltpu.make_async_remote_copy(
-        src_ref=half_send, dst_ref=half_recv, send_sem=half_sem.at[0], recv_sem=half_sem.at[1],
-        device_id=(group, sibling), device_id_type=MESH)
-    half_copy.start()
+
+    @pl.when(core == 1)
+    def _():
+        half_send[...] = act_part
+        half_copy.start()
 
     halves = []
     for h in range(2):
@@ -164,23 +201,15 @@
     own_rows = pl.ds(pl.multiple_of(me * BLOCK_ROWS, BLOCK_ROWS), BLOCK_ROWS)
     grads[own_rows, :] = flat_rows().astype(jnp.bfloat16)
 
-    half_copy.wait()
-    slots[chip] = jnp.where(core == 0, act_part, grad_part) + half_recv[...]
-
-    def slot_copy(shift, source_chip, send, recv):
-        return pltpu.make_async_remote_copy(
-            src_ref=slots.at[source_chip], dst_ref=slots.at[source_chip], send_sem=send, recv_sem=recv,
-            device_id=(group, 2 * peer(shift) + core), device_id_type=MESH)
+    @pl.when(core == 0)
+    def _():
+        share(act_part)
 
     def grad_copy(owner, target, send, recv):
         rows = pl.ds(pl.multiple_of(owner * BLOCK_ROWS, BLOCK_ROWS), BLOCK_ROWS)
         return pltpu.make_async_remote_copy(
             src_ref=grads.at[rows, :], dst_ref=grads.at[rows, :], send_sem=send, recv_sem=recv,
             device_id=(group, target), device_id_type=MESH)
-
-    @pl.loop(1, chips)
-    def _(shift):
-        slot_copy(shift, chip, slot_send.at[shift], slot_recv.at[shift]).start()
 
     grad_copy(me, sibling, own_sem.at[0], own_sem.at[1]).start()
 
@@ -250,17 +279,16 @@
     col_ids = lax.broadcasted_iota(jnp.int32, (ex, cols_all), 1)
     diagonal = row_ids == col_ids
     similarity = jnp.where(diagonal, 0.0, products)
-    sim_out[...] = similarity
     norm_col = jnp.sum(jnp.where(diagonal, products, 0.0), axis=1, keepdims=True) / rank
     own_prompt = jnp.concatenate(
         [jnp.full((1, cols_all), prompts[me * ex + e], jnp.int32) for e in range(ex)], axis=0)
     same = own_prompt == prompt_row[...]
     dup_col = jnp.sum(jnp.where(same, similarity * similarity, 0.0), axis=1, keepdims=True)
-    small_row = lax.broadcasted_iota(jnp.int32, (ex, ex), 0)
-    small_col = lax.broadcasted_iota(jnp.int32, (ex, ex), 1)
-    norm_out[...] = jnp.sum(jnp.where(small_row == small_col, norm_col, 0.0), axis=0, keepdims=True)
-    dup_out[...] = jnp.sum(jnp.where(small_row == small_col, dup_col, 0.0), axis=0, keepdims=True)
-
+    extra = lax.broadcasted_iota(jnp.int32, (ex, result.shape[1] - cols_all), 1)
+    result[...] = jnp.concatenate(
+        [similarity, jnp.where(extra == 0, norm_col, jnp.where(extra == 1, dup_col, 0.0))], axis=1)
+
+    half_copy.wait_send()
     grad_copy(me, sibling, own_sem.at[0], own_sem.at[1]).wait_send()
 
     @pl.loop(1, chips)
@@ -277,22 +305,19 @@
     rank = proj_in.shape[1]
     ex = token_counts.shape[0]
     chips = n // 2
-    chunk = 2048
-    loads = -(-wide // chunk) + -(-model // chunk)
+    chunk = 4096
+    loads = len(plan(wide, chunk)) + len(plan(model, chunk))
     folded = (rank // 2, 2 * rank)
     dma = pltpu.SemaphoreType.DMA
     f32, bf16 = jnp.float32, jnp.bfloat16
     whole = pl.BlockSpec(memory_space=pltpu.VMEM)
     far = pl.BlockSpec(memory_space=pltpu.HBM)
-    similarity, self_norm, dup_score = pl.pallas_call(
+    width = -(-(n * ex + 2) // 128) * 128
+    packed = pl.pallas_call(
         functools.partial(kernel, n, chunk),
-        out_shape=(
-            jax.ShapeDtypeStruct((ex, n * ex), f32),
-            jax.ShapeDtypeStruct((1, ex), f32),
-            jax.ShapeDtypeStruct((1, ex), f32),
-        ),
+        out_shape=jax.ShapeDtypeStruct((ex, width), f32),
         in_specs=[far] * 7,
-        out_specs=(whole, whole, whole),
+        out_specs=whole,
         scratch_shapes=[
             pltpu.VMEM((tok, wide), bf16),
             pltpu.VMEM((tok, model), bf16),
@@ -318,7 +343,7 @@
             flops=2 * tok * (wide + model) * rank, bytes_accessed=2 * tok * (wide + model), transcendentals=0),
     )(*[pltpu.with_memory_space_constraint(x, pltpu.HBM) for x in (
         hidden, cotangent, proj_in.T, proj_out.T, token_counts, loss_mask, prompt_ids)])
-    return similarity, self_norm.reshape(ex), dup_score.reshape(ex)
+    return packed[:, :n * ex], packed[:, n * ex], packed[:, n * ex + 1]
 
 
 def solution(mesh):

time: 25.8 us -> 25.3 us (0.981)
  local copies, waits for them, and re-layouts: 1.6 us -> 1.31 us
    unnamed x3 -> x1, local copies, waits for them, and re-layouts: 1.6 us -> 0.58 us
    slice x0 -> x1, local copies, waits for them, and re-layouts: none -> 0.73 us  [local(): return (packed[:, :n * ex], packed[:, n * ex], packed[:, n * ex + 1])]
where the time goes in v4:
time: 25.3 us; the launch traced here: 25.2 us
  Pallas kernels  23.2 us (92%)
  local copies, waits for them, and re-layouts  1.31 us (5%)
  between operations  0.64 us (3%)
    pallas_call x1, Pallas kernels, local(): pl.pallas_call(functools.partial(kernel, n, chunk), out_shape=jax.ShapeDt...  23.2 us
    slice x1, local copies, waits for them, and re-layouts, local(): return (packed[:, :n * ex], packed[:, n * ex], packed[:, n * ex + 1])  0.73 us
    unnamed x1, local copies, waits for them, and re-layouts  0.58 us

profile of v4, /device:TPU:1, one launch (start us, length us, event | category | flops | bytes accessed | tf_op | source)
XLA Modules:
  0.0 25.2 jit_solution(12610471124494689469)
XLA Ops:
  0.6 23.2 %shard_map.94 = f32[4,128]{1,0:T(4,128)S(1)} custom-call(bf16[256,14336]{1,0:T(8,128)(2,1)} %hidden.1, bf16[256,4096]{1,0:T(8,128)(2,1)} %cotangent.1, bf16[64,14336]{1,0:T(8,128)(2,1)} %bitcast.4, bf16[64,4096]{1,0:T(8,128)(2,1)} %bitcast.5, s32[4]{0:T(128)} %counts_far.1, s32[256]{0:T(256)} %loss_far.1, s32[64]{0:T(128)} %prompts_far.1), custom_call_target="tpu_custom_call" | custom-call | flops 603979776 | bytes 9437184 | tf_op jit(solution)/shard_map/pallas_call | solution.py:316
  23.9 0.7 %slice_reduce_fusion = (f32[4]{0:T(128)}, f32[4]{0:T(128)}) fusion(f32[4,128]{1,0:T(4,128)S(1)} %shard_map.94), kind=kLoop, calls=%fused_computation | loop fusion | bytes 64 | tf_op jit(solution)/shard_map/slice | solution.py:346
  24.6 0.6 %copy.11 = f32[4,64]{1,0:T(4,128)} copy(f32[4,64]{1,0:T(4,128)S(1)} %bitcast.3) | data formatting | bytes 2048
